TPU v7x, 256 devices: a whole 4x4x8 slice. The times are simulated.
256 devices in a mesh: dp: 8 (over z_hi, core), seq: 32 (over y, z_lo, x).
Axes of the slice: x: 4, y: 4, z: 8 (z_hi: 4, z_lo: 2; z = z_hi * 2 + z_lo), core: 2. Of those that a mesh axis runs over, the one named last changes fastest.
Arguments:
- frames: bfloat16 [8, 4096, 1536], P('dp', 'seq'), may hold values from -6 to 6
- w_qkv: bfloat16 [1536, 2304], P('seq'), may hold values from -0.26791294 to 0.26791294
- w_out: bfloat16 [768, 1536], P('seq'), may hold values from -0.21875 to 0.21875
- norm_gains: float32 [2, 1536], replicated, may hold values from 0.1 to 1.9
- conv_kernel: float32 [31, 1536], replicated, may hold values from -1 to 1
- conv_bias: float32 [1536], replicated, may hold values from -3 to 3
- out_grad: bfloat16 [8, 4096, 1536], P('dp', 'seq'), may hold values from -6 to 6
Outputs:
- block_out: bfloat16 [8, 4096, 1536], P('dp', 'seq')
- grad_input: bfloat16 [8, 4096, 1536], P('dp', 'seq')
- grad_qkv: bfloat16 [1536, 2304], P('seq')
- grad_out: bfloat16 [768, 1536], P('seq')
- grad_norms: float32 [2, 1536], replicated
- grad_kernel: float32 [31, 1536], replicated
- grad_bias: float32 [1536], replicated
All inputs are finite; a program needn't handle non-finite values.
Results may differ from a plain program's by a relative error of at most 0.035.
Values may be sent and summed in bfloat16 or wider, within the bound.
A program may use at most 64 MiB of HBM per device.

v0:
```python
import functools

import jax
import jax.numpy as jnp
from jax import lax
from jax.experimental import pallas as pl
from jax.experimental.pallas import tpu as pltpu
from jax.sharding import PartitionSpec as P

EPS = 1e-05
GROUPS = 4
PLANE = 8
HEADS = 3
HD = 64
F32 = jnp.float32
BF16 = jnp.bfloat16


def layer_norm(values, gain):
    center = values - jnp.mean(values, axis=-1, keepdims=True)
    spread = jnp.mean(center * center, axis=-1, keepdims=True)
    inverse = lax.rsqrt(spread + EPS)
    normed = center * inverse
    return (normed * gain, normed, inverse)


def norm_back(grad, normed, inverse, gain):
    scaled = grad * gain
    inner = (
        scaled
        - jnp.mean(scaled, axis=-1, keepdims=True)
        - normed * jnp.mean(scaled * normed, axis=-1, keepdims=True)
    )
    return (inverse * inner, jnp.sum(grad * normed, axis=0))


def dot(a, b, ca, cb):
    return lax.dot_general(a, b, (((ca,), (cb,)), ((), ())), preferred_element_type=F32)


class Place:
    def __init__(self):
        seq = lax.axis_index("seq")
        y, z, x = seq // 8, (seq // 4) % 2, seq % 4
        right, left, far, other = (x + 1) % 4, (x + 3) % 4, (x + 2) % 4, 1 - z
        self.y, self.yp, self.ym, self.yf = y, (y + 1) % 4, (y + 3) % 4, (y + 2) % 4
        self.me = z * 4 + x
        self.xp, self.xm, self.xf = z * 4 + right, z * 4 + left, z * 4 + far
        self.zo = other * 4 + x
        self.zxp, self.zxm, self.zxf = other * 4 + right, other * 4 + left, other * 4 + far

        self.seq, self.dp = seq, lax.axis_index("dp")
        self.core, self.hi = self.dp % 2, self.dp // 2

    def plane(self, p):
        return {"seq": self.y * 8 + p}

    def holder(self, y, dp):
        return {"seq": y * 8 + self.me, "dp": dp}

    def greet(self):
        barrier = pltpu.get_barrier_semaphore()
        near = [{"seq": (self.seq + i) % 32} for i in range(1, 32)]
        near += [
            self.holder((self.y + i) % 4, (self.dp + j) % 8) for i in range(4) for j in range(1, 8)
        ]
        for device in near:
            pl.semaphore_signal(barrier, inc=1, device_id=device)
        pl.semaphore_wait(barrier, len(near))

    def column(self, y):
        return {"seq": y * 8 + self.me}


class Wire:
    def __init__(self, sems):
        self.sems, self.sent = sems, {}

    def go(self, k, src, dst, device):
        copy = pltpu.make_async_remote_copy(
            src_ref=src,
            dst_ref=dst,
            send_sem=self.sems.at[0, k],
            recv_sem=self.sems.at[1, k],
            device_id=device,
        )
        copy.start()
        self.sent[k] = copy

    def got(self, *ks):
        for k in ks:
            self.sent[k].wait_recv()

    def done(self):
        for copy in self.sent.values():
            copy.wait_send()


def wire_sems(count):
    return pltpu.SemaphoreType.DMA((2, count))


class ColumnGather(Wire):
    def __init__(self, sems, place, buf):
        super().__init__(sems)
        self.at, self.buf = place, buf
        self.half = buf.shape[1] // 2

    def begin(self):
        t, own = self.at, self.buf.at[self.at.y]
        self.go(0, own, own, t.column(t.yp))
        self.go(1, own, own, t.column(t.ym))

    def relay(self):
        t, h = self.at, self.half
        self.got(0)
        first = self.buf.at[t.ym, pl.ds(0, h)]
        self.go(2, first, first, t.column(t.yp))
        self.got(1)
        second = self.buf.at[t.yp, pl.ds(h, h)]
        self.go(3, second, second, t.column(t.ym))

    def finish(self):
        self.got(2, 3)


class ColumnReduce(Wire):
    def __init__(self, sems, place, part, relays, lands):
        super().__init__(sems)
        self.at, self.part, self.relays, self.lands = place, part, relays, lands
        self.half = part.shape[1] // 2

    def far(self):
        t, h = self.at, self.half
        self.go(0, self.part.at[t.yf, pl.ds(0, h)], self.relays.at[0], t.column(t.ym))
        self.go(1, self.part.at[t.yf, pl.ds(h, h)], self.relays.at[1], t.column(t.yp))

    def near(self):
        t, h = self.at, self.half
        low, high = pl.ds(0, h), pl.ds(h, h)
        self.go(2, self.part.at[t.ym, high], self.lands.at[0, high], t.column(t.ym))
        self.go(3, self.part.at[t.yp, low], self.lands.at[1, low], t.column(t.yp))

    def relay(self):
        t, h = self.at, self.half
        low, high = pl.ds(0, h), pl.ds(h, h)
        self.got(0)
        self.part[t.ym, low] = (
            self.part[t.ym, low].astype(F32) + self.relays[0].astype(F32)
        ).astype(BF16)
        self.go(4, self.part.at[t.ym, low], self.lands.at[0, low], t.column(t.ym))
        self.got(1)
        self.part[t.yp, high] = (
            self.part[t.yp, high].astype(F32) + self.relays[1].astype(F32)
        ).astype(BF16)
        self.go(5, self.part.at[t.yp, high], self.lands.at[1, high], t.column(t.yp))

    def finish(self):
        self.got(2, 3, 4, 5)
        return (
            self.part[self.at.y].astype(F32)
            + self.lands[0].astype(F32)
            + self.lands[1].astype(F32)
        )


class PlaneGather(Wire):
    def __init__(self, sems, place, full, half):
        super().__init__(sems)
        self.at, self.full, self.half = place, full, half

    def begin(self):
        t, own = self.at, self.full(self.at.me)
        self.go(0, own, own, t.plane(t.xp))
        self.go(1, own, own, t.plane(t.xm))
        self.go(2, own, own, t.plane(t.zo))

    def relay(self):
        t = self.at
        self.got(0)
        first = self.half(t.xm, 0)
        self.go(3, first, first, t.plane(t.xp))
        self.got(1)
        second = self.half(t.xp, 1)
        self.go(4, second, second, t.plane(t.xm))
        self.got(2)
        other = self.full(t.zo)
        self.go(5, other, other, t.plane(t.xp))
        self.go(6, other, other, t.plane(t.xm))

    def cross(self):
        t = self.at
        for k in (0, 1):
            self.got(3 + k)
            part = self.half(t.xf, k)
            self.go(7 + k, part, part, t.plane(t.zo))

    def finish(self):
        self.got(5, 6, 7, 8)


class PlaneReduce(Wire):
    def __init__(self, sems, place, full, half, land, half_land):
        super().__init__(sems)
        self.at, self.full, self.half = place, full, half
        self.land, self.half_land = land, half_land

    def add(self, ref, *more):
        total = ref[...].astype(F32)
        for other in more:
            total = total + other[...].astype(F32)
        ref[...] = total.astype(BF16)

    def far(self):
        t = self.at
        self.go(0, self.full(t.zxf), self.land(0), t.plane(t.zo))

    def sides(self):
        t = self.at
        self.go(1, self.full(t.zxm), self.land(1), t.plane(t.xm))
        self.go(2, self.full(t.zxp), self.land(2), t.plane(t.xp))

    def opposite(self):
        t = self.at
        self.got(0)
        self.add(self.full(t.xf), self.land(0))
        self.go(3, self.half(t.xf, 0), self.half_land(0), t.plane(t.xm))
        self.go(4, self.half(t.xf, 1), self.half_land(1), t.plane(t.xp))

    def across(self):
        t = self.at
        self.got(1, 2)
        self.add(self.full(t.zo), self.land(1), self.land(2))
        self.go(5, self.full(t.zo), self.land(3), t.plane(t.zo))

    def near(self):
        t = self.at
        self.got(3)
        self.add(self.half(t.xm, 0), self.half_land(0))
        self.go(6, self.full(t.xm), self.land(4), t.plane(t.xm))
        self.got(4)
        self.add(self.half(t.xp, 1), self.half_land(1))
        self.go(7, self.full(t.xp), self.land(5), t.plane(t.xp))

    def finish(self):
        self.got(5, 6, 7)
        total = self.full(self.at.me)[...].astype(F32)
        for k in (3, 4, 5):
            total = total + self.land(k)[...].astype(F32)
        return total


def pick(i, *values):
    out = values[-1]
    for k in range(len(values) - 2, -1, -1):
        out = jnp.where(i == k, values[k], out)
    return out


def local_copies(pairs, sems):
    copies = [
        pltpu.make_async_copy(src, dst, sems.at[i]) for i, (src, dst) in enumerate(pairs)
    ]
    for copy in copies:
        copy.start()
    return copies


QB = 128


def forward_block(kv, c, h, cols, qpad, top, total, acc):
    both = kv[c, :, h * 128 : (h + 1) * 128]
    scores = dot(both, qpad[h, cols, :], 1, 1)
    old = top[h, :, cols]
    new = jnp.maximum(old, jnp.max(scores, axis=0, keepdims=True))
    shrink = jnp.exp(old - new)
    expo = jnp.exp(scores - new)
    top[h, :, cols] = new
    total[h, :, cols] = total[h, :, cols] * shrink + jnp.sum(expo, axis=0, keepdims=True)
    acc[h, :, cols] = acc[h, :, cols] * shrink + dot(both, expo.astype(BF16), 0, 0)


def forward_chunk(kv, c, qpad, top, total, acc):
    for h in range(HEADS):
        for b in range(qpad.shape[1] // QB):
            forward_block(kv, c, h, slice(b * QB, (b + 1) * QB), qpad, top, total, acc)


def backward_chunk(kv, c, qpad, dopad, lse, delta, dqt, out):
    for h in range(HEADS):
        lanes = slice(h * 128, (h + 1) * 128)
        both, query, grad = kv[c, :, lanes], qpad[h], dopad[h]
        scores = dot(both, query, 1, 1)
        slopes = dot(both, grad, 1, 1)
        probs = jnp.exp(scores - lse[h])
        score_grads = (probs * (slopes - delta[h])).astype(BF16)
        out[c, :, lanes] = (
            dot(probs.astype(BF16), grad, 1, 0) + dot(score_grads, query, 1, 0)
        ).astype(BF16)
        dqt[h] += dot(both, score_grads, 0, 0)


HALO = 16
LANES = 128


def shifts(wide, length, taps):
    for low in range(8):
        moved = wide if low == 0 else pltpu.roll(wide, wide.shape[0] - low, 0)
        for offset in range(low, taps + 1, 8):
            if offset > 0:
                yield offset, moved[offset - low : offset - low + length]


class Edge(Wire):
    def __init__(self, sems, place, wide):
        super().__init__(sems)
        t, rows = place, wide.shape[0]
        self.first, self.last = t.seq == 0, t.seq == 31
        nothing = jnp.zeros((HALO, wide.shape[1]), BF16)

        @pl.when(self.first)
        def _():
            wide[0:HALO] = nothing

        @pl.when(self.last)
        def _():
            wide[rows - HALO :] = nothing

        self.up = pltpu.make_async_remote_copy(
            src_ref=wide.at[pl.ds(rows - 2 * HALO, HALO)],
            dst_ref=wide.at[pl.ds(0, HALO)],
            send_sem=sems.at[0, 0],
            recv_sem=sems.at[1, 0],
            device_id={"seq": jnp.minimum(t.seq + 1, 31)},
        )
        self.down = pltpu.make_async_remote_copy(
            src_ref=wide.at[pl.ds(HALO, HALO)],
            dst_ref=wide.at[pl.ds(rows - HALO, HALO)],
            send_sem=sems.at[0, 1],
            recv_sem=sems.at[1, 1],
            device_id={"seq": jnp.maximum(t.seq - 1, 0)},
        )

    def begin(self):
        @pl.when(jnp.logical_not(self.last))
        def _():
            self.up.start()

        @pl.when(jnp.logical_not(self.first))
        def _():
            self.down.start()

    def finish(self):
        @pl.when(jnp.logical_not(self.last))
        def _():
            self.up.wait_send()
            self.down.wait_recv()

        @pl.when(jnp.logical_not(self.first))
        def _():
            self.down.wait_send()
            self.up.wait_recv()


def whole_kernel(names, *refs):
    r = dict(zip(names, refs))
    (
        frames,
        w_qkv,
        w_out,
        gains_in,
        conv_kernel,
        conv_bias,
        out_grad,
        block_out,
        grad_input,
        grad_qkv,
        grad_out,
        kernel_sum,
        bias_sum,
        norms_sum,
        w_parts,
        hid,
        wq,
        wo,
        wo32,
        wo16,
        kv,
        qpad,
        lse,
        total,
        acc,
        att,
        part,
        relays,
        lands,
        mixed_keep,
        normed_keep,
        conv_wide,
        grad_wide,
        conv_back,
        mix,
        dopad,
        delta,
        dqt,
        dkv,
        kv_land,
        kv_half,
        proj,
        part2,
        relays2,
        lands2,
        w_part,
        w_core,
        w_land,
        w_half,
        w_hi,
        w_done,
        w_fin,
        o_part,
        o_core,
        o_land,
        o_half,
        o_hi,
        o_done,
        o_fin,
        s_send,
        s_seq,
        s_mine,
        s_dp,
        s_done,
        s_fin,
        spread_sems,
        hid_sems,
        wq_sems,
        wo_sems,
        gather_sems,
        sum_sems,
        conv_sems,
        grad_sems,
        mix_sems,
        kv_sems,
        red_sems,
        core_sems,
        w_sems,
        o_sems,
        hi_sems,
        w_fin_send,
        w_fin_recv,
        o_fin_send,
        o_fin_recv,
        s_sems,
        s_dp_sems,
        s_fin_sems,
    ) = (r[n] for n in names)
    t = Place()
    t.greet()
    rows, model = frames.shape
    many = GROUPS * rows
    width = HEADS * HD
    shard = w_qkv.shape[0]
    gain1, gain2 = gains_in[0:1, :], gains_in[1:2, :]

    for g in range(GROUPS):
        columns = [w_qkv[:, g * width : (g + 1) * width]]
        for h in range(HEADS):
            for kind in (1, 2):
                start = (kind * GROUPS + g) * width + h * HD
                columns.append(w_qkv[:, start : start + HD])
        w_parts[g] = jnp.concatenate(columns, axis=1)
    spread = Wire(spread_sems)
    for k, y in enumerate((t.yp, t.ym, t.yf)):
        spread.go(k, w_parts.at[y], wq.at[t.y, t.me], t.column(y))
    wq[t.y, t.me] = w_parts[t.y]
    share = width // PLANE
    wo[t.me] = jnp.concatenate(
        [w_out[...].astype(F32), jnp.zeros((wo.shape[1] - share, model), F32)], axis=0
    ).astype(BF16)

    inputs = frames[...].astype(F32)
    shifted, _, _ = layer_norm(inputs, gain1)
    hid[t.y] = shifted.astype(BF16)
    hid_net = ColumnGather(hid_sems, t, hid)
    hid_net.begin()
    spread.got(0, 1, 2)
    wq_net = PlaneGather(
        wq_sems, t, lambda p: wq.at[:, p], lambda p, i: wq.at[pl.ds(2 * i, 2), p]
    )
    wo_net = PlaneGather(
        wo_sems, t, lambda p: wo.at[p], lambda p, i: wo.at[p, pl.ds(16 * i, 16)]
    )
    wq_net.begin()
    hid_net.relay()
    wq_net.relay()
    wq_net.cross()
    wo_net.begin()
    hid_net.finish()
    wq_net.finish()

    hidden = hid[...].reshape(many, model)
    weights = wq[...].reshape(model, 3 * width)
    projected = dot(hidden, weights, 1, 0).astype(BF16)
    kv[t.me] = projected[:, width:]
    kv_net = PlaneGather(
        gather_sems,
        t,
        lambda p: kv.at[p],
        lambda p, i: kv.at[p, pl.ds(i * (many // 2), many // 2)],
    )
    kv_net.begin()
    zeros = jnp.zeros((many, HD), BF16)
    for h in range(HEADS):
        qpad[h] = jnp.concatenate(
            [projected[:, h * HD : (h + 1) * HD] * BF16(HD**-0.5), zeros], axis=1
        )
    lse[...] = jnp.full_like(lse, -jnp.inf)
    total[...] = jnp.zeros_like(total)
    acc[...] = jnp.zeros_like(acc)

    def attend(*chunks):
        if len(chunks) == 1:
            forward_chunk(kv, chunks[0], qpad, lse, total, acc)
            return

        def step(i, carry):
            forward_chunk(kv, pick(i, *chunks), qpad, lse, total, acc)
            return carry

        lax.fori_loop(0, len(chunks), step, 0)

    attend(t.me)
    kv_net.relay()
    wo_net.relay()
    attend(t.xm, t.xp, t.zo)
    kv_net.cross()
    wo_net.cross()
    attend(t.xf)
    wo_net.finish()
    for p in range(PLANE):
        wo32[p * share : (p + 1) * share, :] = wo[p, 0:share, :].astype(F32)
    wo16[...] = wo32[...].astype(BF16)
    kv_net.got(5, 6)
    kv_net.got(7, 8)

    def last(y):
        cols = pl.ds(pl.multiple_of(y * rows, rows), rows)

        def step(i, carry):
            c = pick(i, t.zxm, t.zxp, t.zxf)
            for h in range(HEADS):
                forward_block(kv, c, h, cols, qpad, lse, total, acc)
            return carry

        lax.fori_loop(0, 3, step, 0)
        blocks = []
        for h in range(HEADS):
            blocks.append((acc[h, HD : 2 * HD, cols] / total[h, :, cols]).T.astype(BF16))
            lse[h, :, cols] = lse[h, :, cols] + jnp.log(total[h, :, cols])
        here = jnp.concatenate(blocks, axis=1)
        att[cols, :] = here
        part[y] = dot(here, wo16[...], 1, 0).astype(BF16)

    sum_net = ColumnReduce(sum_sems, t, part, relays, lands)
    last(t.yf)
    sum_net.far()
    last(t.ym)
    last(t.yp)
    sum_net.near()
    last(t.y)
    sum_net.relay()
    mixed = (frames[...].astype(F32) + sum_net.finish()).astype(BF16)

    mixed32 = mixed.astype(F32)
    mixed_keep[...] = mixed32
    shifted, normed, inverse = layer_norm(mixed32, gain2)
    inside = slice(HALO, HALO + rows)
    conv_wide[inside] = shifted.astype(BF16)
    conv_edge = Edge(conv_sems, t, conv_wide)
    conv_edge.begin()
    normed_keep[...] = normed
    conv_edge.finish()
    taps = conv_kernel.shape[0]

    def lanes_of(b):
        return pl.ds(pl.multiple_of(b * LANES, LANES), LANES)

    def convolve(b, carry):
        lanes = lanes_of(b)
        pre = jnp.zeros((rows, LANES), F32) + conv_bias[:, lanes]
        for offset, moved in shifts(conv_wide[:, lanes].astype(F32), rows, taps):
            pre = pre + moved * conv_kernel[offset - 1 : offset, lanes]
        sigma = 1.0 / (1.0 + jnp.exp(-pre))
        block_out[:, lanes] = (mixed_keep[:, lanes] + pre * sigma).astype(BF16)
        grad_wide[inside, lanes] = (
            out_grad[:, lanes].astype(F32) * sigma * (1.0 + pre * (1.0 - sigma))
        ).astype(BF16)
        return carry

    blocks = model // LANES
    lax.fori_loop(0, blocks, convolve, 0)
    grad_edge = Edge(grad_sems, t, grad_wide)
    grad_edge.begin()
    grad_edge.finish()

    def convolve_back(b, carry):
        lanes = lanes_of(b)
        grad = jnp.zeros((rows, LANES), F32)
        for offset, moved in shifts(grad_wide[:, lanes].astype(F32), rows, taps):
            grad = grad + moved * conv_kernel[taps - offset : taps - offset + 1, lanes]
        conv_back[:, lanes] = grad
        return carry

    lax.fori_loop(0, blocks, convolve_back, 0)
    norm_grad, gain2_grad = norm_back(conv_back[...], normed_keep[...], inverse, gain2)
    gain2_grad = gain2_grad[None]
    mix[t.y] = (out_grad[...].astype(F32) + norm_grad).astype(BF16)
    mix_net = ColumnGather(mix_sems, t, mix)
    mix_net.begin()

    def kernel_grads(b, carry):
        lanes = lanes_of(b)
        grad = grad_wide[inside, lanes].astype(F32)
        for offset, moved in shifts(conv_wide[:, lanes].astype(F32), rows, taps):
            s_send[offset - 1, :, lanes] = jnp.sum(grad * moved, axis=0, keepdims=True)
        s_send[taps, :, lanes] = jnp.sum(grad, axis=0, keepdims=True)
        return carry

    lax.fori_loop(0, blocks, kernel_grads, 0)
    mix_net.relay()
    mix_net.finish()

    mixed = mix[...].reshape(many, model)
    grads = dot(mixed, wo16[...], 1, 1).astype(BF16)
    for h in range(HEADS):
        lanes = slice(h * HD, (h + 1) * HD)
        mine = grads[:, lanes]
        dopad[h] = jnp.concatenate([zeros, mine], axis=1)
        delta[h] = jnp.sum(
            (att[:, lanes].astype(F32) * mine.astype(F32)).T, axis=0, keepdims=True
        )
    dqt[...] = jnp.zeros_like(dqt)

    def backward(*chunks):
        def step(i, carry):
            backward_chunk(kv, pick(i, *chunks), qpad, dopad, lse, delta, dqt, dkv)
            return carry

        if len(chunks) == 1:
            step(0, 0)
        else:
            lax.fori_loop(0, len(chunks), step, 0)

    half = many // 2
    net = PlaneReduce(
        kv_sems,
        t,
        lambda p: dkv.at[p],
        lambda p, i: dkv.at[p, pl.ds(i * half, half)],
        lambda k: kv_land.at[k],
        lambda k: kv_half.at[k],
    )
    backward(t.zxf)
    net.far()
    backward(t.zxm, t.zxp)
    net.sides()
    backward(t.xf)
    net.opposite()
    backward(t.zo)
    net.across()
    backward(t.xm, t.xp)
    net.near()
    backward(t.me)
    for h in range(HEADS):
        proj[:, h * HD : (h + 1) * HD] = (dqt[h, 0:HD, :] * HD**-0.5).T.astype(BF16)

    out_terms = dot(att[...], mixed, 0, 0)
    quarter = o_part.shape[2]
    wide = model // 2
    for c in range(2):
        for p in range(PLANE):
            for i in range(quarter):
                piece = o_part.at[c, p, i]
                if i * 8 < share:
                    start = p * share + i * 8
                    piece[...] = out_terms[
                        start : start + 8, c * wide : (c + 1) * wide
                    ].astype(BF16)
                else:
                    piece[...] = jnp.zeros(piece.shape, BF16)
    order = (t.zxf, t.zxm, t.zxp, t.xf, t.zo, t.xm, t.xp, t.me)
    buddy = {"dp": t.hi * 2 + 1 - t.core}
    pair = Wire(core_sems)
    for k, p in enumerate(order):
        pair.go(k, o_part.at[1 - t.core, p], o_core.at[p], buddy)
    proj[:, width:] = net.finish().astype(BF16)

    weights = wq[...].reshape(model, 3 * width)

    def product(y):
        here = proj[pl.ds(pl.multiple_of(y * rows, rows), rows), :]
        part2[y] = dot(here, weights, 1, 1).astype(BF16)

    red = ColumnReduce(red_sems, t, part2, relays2, lands2)
    product(t.yf)
    red.far()
    hidden = hid[...].reshape(many, model)
    half_rows = w_part.shape[3]
    w_terms = dot(hidden, proj[...], 0, 0).reshape(
        GROUPS, PLANE, 2, half_rows, 3 * width
    )
    for c in range(2):
        w_part[c] = w_terms[:, :, c].astype(BF16)
    for k, p in enumerate(order):
        pair.go(8 + k, w_part.at[1 - t.core, :, p], w_core.at[:, p], buddy)
    w_mine, o_mine = w_part.at[t.core], o_part.at[t.core]
    o_net = PlaneReduce(
        o_sems,
        t,
        lambda p: o_mine.at[p],
        lambda p, i: o_mine.at[p, pl.ds(2 * i, 2)],
        lambda k: o_land.at[k],
        lambda k: o_half.at[k],
    )
    w_net = PlaneReduce(
        w_sems,
        t,
        lambda p: w_mine.at[:, p],
        lambda p, i: w_mine.at[pl.ds(2 * i, 2), p],
        lambda k: w_land.at[k],
        lambda k: w_half.at[k],
    )

    def join(first, last):
        for k in range(first, last):
            p = order[k]
            pair.got(k, 8 + k)
            o_net.add(o_mine.at[p], o_core.at[p])
            w_net.add(w_mine.at[:, p], w_core.at[:, p])

    product(t.ym)
    product(t.yp)
    product(t.y)
    red.near()
    red.relay()
    join(0, 1)
    w_net.far()
    o_net.far()
    join(1, 3)
    w_net.sides()
    o_net.sides()
    join(3, 8)
    w_net.opposite()
    o_net.opposite()
    w_net.across()
    o_net.across()
    w_net.near()
    o_net.near()

    grad_hidden = red.finish()
    _, normed, inverse = layer_norm(frames[...].astype(F32), gain1)
    norm_grad, gain_sum = norm_back(grad_hidden, normed, inverse, gain1)
    grad_input[...] = (mix[t.y].astype(F32) + norm_grad).astype(BF16)
    gains = (gain_sum[None], gain2_grad)
    count = s_send.shape[0]
    for r in range(count):
        if r < 2 * (model // 128):
            row, col = divmod(r, model // 128)
            s_send[r, :, model:] = gains[row][:, col * 128 : (col + 1) * 128]
        else:
            s_send[r, :, model:] = jnp.zeros((1, 128), F32)
    s_net = Wire(s_sems)
    s_seq[t.seq] = s_send[t.seq]
    for k in range(1, count):
        r = (t.seq + k) % count
        s_net.go(k - 1, s_send.at[r], s_seq.at[t.seq], {"seq": r})

    o_total, w_total = o_net.finish(), w_net.finish()
    o_mine[t.me] = o_total.astype(BF16)
    w_mine[:, t.me] = w_total.astype(BF16)
    hi_net = Wire(hi_sems)
    for k in range(1, 4):
        j = (t.hi + k) % 4
        there = {"dp": j * 2 + t.core}
        hi_net.go(k - 1, w_mine.at[j, t.me], w_hi.at[k - 1], there)
        hi_net.go(2 + k, o_mine.at[t.me, j], o_hi.at[k - 1], there)

    s_net.got(*range(count - 1))
    s_mine[...] = jnp.sum(s_seq[...], axis=0)
    s_dp[t.dp] = s_mine[...]
    s_dp_net = Wire(s_dp_sems)
    for k in range(1, 8):
        s_dp_net.go(k - 1, s_mine, s_dp.at[t.dp], {"dp": (t.dp + k) % 8})

    hi_net.got(*range(6))
    w_out_block = w_mine[t.hi, t.me].astype(F32)
    o_out_block = o_mine[t.me, t.hi].astype(F32)
    for k in range(3):
        w_out_block = w_out_block + w_hi[k].astype(F32)
        o_out_block = o_out_block + o_hi[k].astype(F32)
    w_done[...] = w_out_block.astype(BF16)
    o_done[...] = o_out_block.astype(BF16)
    finals = []
    for k in range(1, 8):
        d = (t.dp + k) % 8
        for src, dst, send, recv, y in (
            (w_done, w_fin.at[t.y, t.core], w_fin_send.at[k], w_fin_recv.at[t.y, t.core], t.hi),
            (o_done, o_fin.at[t.hi, t.core], o_fin_send.at[k], o_fin_recv.at[t.hi, t.core], t.y),
        ):
            copy = pltpu.make_async_remote_copy(
                src_ref=src, dst_ref=dst, send_sem=send, recv_sem=recv, device_id=t.holder(y, d)
            )
            copy.start()
            finals.append(copy)
    o_own = pltpu.make_async_copy(
        o_done, o_fin.at[t.hi, t.core], o_fin_recv.at[t.hi, t.core]
    )
    o_own.start()
    w_own = pltpu.make_async_copy(w_done, w_fin.at[t.y, t.core], w_fin_recv.at[t.y, t.core])
    w_away = pltpu.make_async_remote_copy(
        src_ref=w_done,
        dst_ref=w_fin.at[t.y, t.core],
        send_sem=w_fin_send.at[0],
        recv_sem=w_fin_recv.at[t.y, t.core],
        device_id=t.holder(t.hi, t.dp),
    )

    @pl.when(t.hi == t.y)
    def _():
        w_own.start()

    @pl.when(t.hi != t.y)
    def _():
        w_away.start()

    s_dp_net.got(*range(7))
    summed = s_dp[0]
    for d in range(1, 8):
        summed = summed + s_dp[d]
    s_done[...] = summed
    s_fin[t.seq] = summed
    s_fin_net = Wire(s_fin_sems)
    for k in range(1, count):
        s_fin_net.go(k - 1, s_done, s_fin.at[t.seq], {"seq": (t.seq + k) % count})

    for i in range(4):
        for c in range(2):
            pltpu.make_async_copy(w_done, w_fin.at[i, c], w_fin_recv.at[i, c]).wait()
            pltpu.make_async_copy(o_done, o_fin.at[i, c], o_fin_recv.at[i, c]).wait()
    pieces = [w_fin[y].astype(F32).reshape(2 * half_rows, 3 * width) for y in range(GROUPS)]
    columns = [piece[:, :width] for piece in pieces]
    for kind in range(2):
        for piece in pieces:
            for h in range(HEADS):
                start = width + (2 * h + kind) * HD
                columns.append(piece[:, start : start + HD])
    grad_qkv[...] = jnp.concatenate(columns, axis=1).astype(BF16)
    sides = [
        o_fin[0 : share // 8, c].astype(F32).reshape(share, wide) for c in range(2)
    ]
    grad_out[...] = jnp.concatenate(sides, axis=1).astype(BF16)
    s_fin_net.got(*range(count - 1))
    for r in range(count):
        row = s_fin[r]
        if r < taps:
            kernel_sum[r : r + 1, :] = row[:, :model]
        else:
            bias_sum[...] = row[:, :model]
        if r < 2 * (model // 128):
            i, col = divmod(r, model // 128)
            norms_sum[i : i + 1, col * 128 : (col + 1) * 128] = row[:, model:]
    for copy in finals:
        copy.wait_send()

    @pl.when(t.hi != t.y)
    def _():
        w_away.wait_send()

    for wire in (spread, hid_net, wq_net, wo_net, kv_net, sum_net, mix_net, net, pair, o_net, red, w_net, hi_net, s_net, s_dp_net, s_fin_net):
        wire.done()


def bf16(*shape):
    return pltpu.VMEM(shape, BF16)


def f32(*shape):
    return pltpu.VMEM(shape, F32)


def dma(*shape):
    return pltpu.SemaphoreType.DMA(shape)


def whole(frames, w_qkv, w_out, gains, conv_kernel, conv_bias, out_grad):
    rows, model = frames.shape
    shard = w_qkv.shape[0]
    many = GROUPS * rows
    width = HEADS * HD
    half = shard // 2
    padded = 32
    count = conv_kernel.shape[0] + 1
    like = jax.ShapeDtypeStruct
    ins = dict(
        frames=frames,
        w_qkv=w_qkv,
        w_out=w_out,
        gains_in=gains,
        conv_kernel=conv_kernel,
        conv_bias=conv_bias,
        out_grad=out_grad,
    )
    outs = dict(
        block_out=like((rows, model), BF16),
        grad_input=like((rows, model), BF16),
        grad_qkv=like(w_qkv.shape, BF16),
        grad_out=like(w_out.shape, BF16),
        kernel_sum=like((count - 1, model), F32),
        bias_sum=like((1, model), F32),
        norms_sum=like((2, model), F32),
    )
    scratch = dict(
        w_parts=bf16(GROUPS, shard, 3 * width),
        hid=bf16(GROUPS, rows, model),
        wq=bf16(GROUPS, PLANE, shard, 3 * width),
        wo=bf16(PLANE, padded, model),
        wo32=f32(width, model),
        wo16=bf16(width, model),
        kv=bf16(PLANE, many, 2 * width),
        qpad=bf16(HEADS, many, 2 * HD),
        lse=f32(HEADS, 1, many),
        total=f32(HEADS, 1, many),
        acc=f32(HEADS, 2 * HD, many),
        att=bf16(many, width),
        part=bf16(GROUPS, rows, model),
        relays=bf16(2, rows // 2, model),
        lands=bf16(2, rows, model),
        mixed_keep=f32(rows, model),
        normed_keep=f32(rows, model),
        conv_wide=bf16(rows + 2 * HALO, model),
        grad_wide=bf16(rows + 2 * HALO, model),
        conv_back=f32(rows, model),
        mix=bf16(GROUPS, rows, model),
        dopad=bf16(HEADS, many, 2 * HD),
        delta=f32(HEADS, 1, many),
        dqt=f32(HEADS, 2 * HD, many),
        dkv=bf16(PLANE, many, 2 * width),
        kv_land=bf16(6, many, 2 * width),
        kv_half=bf16(2, many // 2, 2 * width),
        proj=bf16(many, 3 * width),
        part2=bf16(GROUPS, rows, model),
        relays2=bf16(2, rows // 2, model),
        lands2=bf16(2, rows, model),
        w_part=bf16(2, GROUPS, PLANE, half, 3 * width),
        w_core=bf16(GROUPS, PLANE, half, 3 * width),
        w_land=bf16(6, GROUPS, half, 3 * width),
        w_half=bf16(2, GROUPS // 2, half, 3 * width),
        w_hi=bf16(3, half, 3 * width),
        w_done=bf16(half, 3 * width),
        w_fin=bf16(GROUPS, 2, half, 3 * width),
        o_part=bf16(2, PLANE, 4, 8, model // 2),
        o_core=bf16(PLANE, 4, 8, model // 2),
        o_land=bf16(6, 4, 8, model // 2),
        o_half=bf16(2, 2, 8, model // 2),
        o_hi=bf16(3, 8, model // 2),
        o_done=bf16(8, model // 2),
        o_fin=bf16(4, 2, 8, model // 2),
        s_send=f32(count, 1, model + LANES),
        s_seq=f32(count, 1, model + LANES),
        s_mine=f32(1, model + LANES),
        s_dp=f32(8, 1, model + LANES),
        s_done=f32(1, model + LANES),
        s_fin=f32(count, 1, model + LANES),
        spread_sems=wire_sems(3),
        hid_sems=wire_sems(4),
        wq_sems=wire_sems(9),
        wo_sems=wire_sems(9),
        gather_sems=wire_sems(9),
        sum_sems=wire_sems(6),
        conv_sems=wire_sems(2),
        grad_sems=wire_sems(2),
        mix_sems=wire_sems(4),
        kv_sems=wire_sems(8),
        red_sems=wire_sems(6),
        core_sems=wire_sems(16),
        w_sems=wire_sems(8),
        o_sems=wire_sems(8),
        hi_sems=wire_sems(6),
        w_fin_send=dma(8),
        w_fin_recv=dma(4, 2),
        o_fin_send=dma(8),
        o_fin_recv=dma(4, 2),
        s_sems=wire_sems(count - 1),
        s_dp_sems=wire_sems(7),
        s_fin_sems=wire_sems(count - 1),
    )
    vmem = pl.BlockSpec(memory_space=pltpu.VMEM)
    names = [*ins, *outs, *scratch]
    return pl.pallas_call(
        functools.partial(whole_kernel, names),
        out_shape=list(outs.values()),
        in_specs=[vmem] * len(ins),
        out_specs=[vmem] * len(outs),
        scratch_shapes=list(scratch.values()),
        compiler_params=pltpu.CompilerParams(
            collective_id=0, has_side_effects=True, vmem_limit_bytes=62 * 2**20
        ),
        name="whole",
    )(*ins.values())


def hand_on_kernel(*refs):
    half = len(refs) // 2
    for src, dst in zip(refs[:half], refs[half:]):
        dst[...] = src[...].reshape(dst.shape)


def hand_on(*arrays):
    vmem = pl.BlockSpec(memory_space=pltpu.VMEM)
    return pl.pallas_call(
        hand_on_kernel,
        out_shape=[jax.ShapeDtypeStruct(a.shape, a.dtype) for a in arrays],
        in_specs=[vmem] * len(arrays),
        out_specs=[vmem] * len(arrays),
        name="hand_on",
    )(*arrays)


def local(frames, w_qkv, w_out, norm_gains, conv_kernel, conv_bias, out_grad):
    block_out, grad_input, grad_qkv, grad_out, kernel_sum, bias_sum, norms_sum = hand_on(
        *whole(
            frames[0], w_qkv, w_out, norm_gains, conv_kernel, conv_bias[None], out_grad[0]
        )
    )
    return (
        block_out[None],
        grad_input[None],
        grad_qkv,
        grad_out,
        norms_sum,
        kernel_sum,
        bias_sum[0],
    )


def solution(mesh):
    in_specs = (
        P("dp", "seq", None),
        P("seq", None),
        P("seq", None),
        P(),
        P(),
        P(),
        P("dp", "seq", None),
    )
    out_specs = (
        P("dp", "seq", None),
        P("dp", "seq", None),
        P("seq", None),
        P("seq", None),
        P(),
        P(),
        P(),
    )
    return jax.shard_map(local, mesh=mesh, in_specs=in_specs, out_specs=out_specs, check_vma=False)
```

profile of v0, /device:TPU:1, one launch (start us, length us, event | category | flops | bytes accessed | tf_op | source)
XLA Modules:
  0.0 189.9 jit_solution(12002712075226214773)
XLA Ops:
  0.6 1.3 broadcast_in_dim.9.refs_5_
  1.9 184.3 %whole.1 = (bf16[128,1536]{1,0:T(8,128)(2,1)}, bf16[128,1536]{1,0:T(8,128)(2,1)}, bf16[48,2304]{1,0:T(8,128)(2,1)}, bf16[24,1536]{1,0:T(8,128)(2,1)}, f32[31,153...) custom-call(bf16[128,1536]{1,0:T(8,128)(2,1)} %bitcast.4, bf16[48,2304]{1,0:T(8,128)(2,1)} %refs_1_.1, ...), custom_call_target="tpu_custom_call" | custom-call | tf_op jit(solution)/shard_map/whole/pallas_call | solution.py:1000
  186.2 2.4 %hand_on.1 = (bf16[128,1536]{1,0:T(8,128)(2,1)}, bf16[128,1536]{1,0:T(8,128)(2,1)}, bf16[48,2304]{1,0:T(8,128)(2,1)}, bf16[24,1536]{1,0:T(8,128)(2,1)}, f32[31,1...) custom-call(bf16[128,1536]{1,0:T(8,128)(2,1)} %get-tuple-element.21.refs_0_, ...), custom_call_target="tpu_custom_call" | custom-call | tf_op jit(solution)/shard_map/hand_on/pallas_call | solution.py:1021
  188.6 0.0 copy-start
  188.6 0.7 copy-done
  189.2 0.6 reduce
Async XLA Ops:
  188.6 0.7 copy-start
where the time goes:
time: 190 us
  Pallas kernels  187 us (98%)
  local copies, waits for them, and re-layouts  1.99 us (1%)
    pallas_call x1, Pallas kernels, whole(): pl.pallas_call(functools.partial(whole_kernel, names), out_shape=list(out...  184 us

commit v1 on v0

--- a/solution.py
+++ b/solution.py
@@ -59,14 +59,13 @@
         return {"seq": y * 8 + self.me, "dp": dp}
 
     def greet(self):
-        barrier = pltpu.get_barrier_semaphore()
         near = [{"seq": (self.seq + i) % 32} for i in range(1, 32)]
         near += [
             self.holder((self.y + i) % 4, (self.dp + j) % 8) for i in range(4) for j in range(1, 8)
         ]
         for device in near:
-            pl.semaphore_signal(barrier, inc=1, device_id=device)
-        pl.semaphore_wait(barrier, len(near))
+            pl.semaphore_signal(pltpu.get_barrier_semaphore(), inc=1, device_id=device)
+        return len(near)
 
     def column(self, y):
         return {"seq": y * 8 + self.me}
@@ -287,16 +286,21 @@
             forward_block(kv, c, h, slice(b * QB, (b + 1) * QB), qpad, top, total, acc)
 
 
-def backward_chunk(kv, c, qpad, dopad, lse, delta, dqt, out):
+def prob_chunk(kv, c, qpad, lse, probs):
+    for h in range(HEADS):
+        scores = dot(kv[c, :, h * 128 : (h + 1) * 128], qpad[h], 1, 1)
+        probs[c, h] = jnp.exp(scores - lse[h]).astype(BF16)
+
+
+def backward_chunk(kv, c, qpad, dopad, probs, delta, dqt, out):
     for h in range(HEADS):
         lanes = slice(h * 128, (h + 1) * 128)
         both, query, grad = kv[c, :, lanes], qpad[h], dopad[h]
-        scores = dot(both, query, 1, 1)
         slopes = dot(both, grad, 1, 1)
-        probs = jnp.exp(scores - lse[h])
-        score_grads = (probs * (slopes - delta[h])).astype(BF16)
+        prob = probs[c, h]
+        score_grads = (prob.astype(F32) * (slopes - delta[h])).astype(BF16)
         out[c, :, lanes] = (
-            dot(probs.astype(BF16), grad, 1, 0) + dot(score_grads, query, 1, 0)
+            dot(prob, grad, 1, 0) + dot(score_grads, query, 1, 0)
         ).astype(BF16)
         dqt[h] += dot(both, score_grads, 0, 0)
 
@@ -393,6 +397,8 @@
         total,
         acc,
         att,
+        hid_turned,
+        probs,
         part,
         relays,
         lands,
@@ -456,7 +462,7 @@
         s_fin_sems,
     ) = (r[n] for n in names)
     t = Place()
-    t.greet()
+    greeted = t.greet()
     rows, model = frames.shape
     many = GROUPS * rows
     width = HEADS * HD
@@ -470,6 +476,12 @@
                 start = (kind * GROUPS + g) * width + h * HD
                 columns.append(w_qkv[:, start : start + HD])
         w_parts[g] = jnp.concatenate(columns, axis=1)
+    inputs = frames[...].astype(F32)
+    shifted, _, _ = layer_norm(inputs, gain1)
+    hid[t.y] = shifted.astype(BF16)
+    pl.semaphore_wait(pltpu.get_barrier_semaphore(), greeted)
+    hid_net = ColumnGather(hid_sems, t, hid)
+    hid_net.begin()
     spread = Wire(spread_sems)
     for k, y in enumerate((t.yp, t.ym, t.yf)):
         spread.go(k, w_parts.at[y], wq.at[t.y, t.me], t.column(y))
@@ -479,11 +491,6 @@
         [w_out[...].astype(F32), jnp.zeros((wo.shape[1] - share, model), F32)], axis=0
     ).astype(BF16)
 
-    inputs = frames[...].astype(F32)
-    shifted, _, _ = layer_norm(inputs, gain1)
-    hid[t.y] = shifted.astype(BF16)
-    hid_net = ColumnGather(hid_sems, t, hid)
-    hid_net.begin()
     spread.got(0, 1, 2)
     wq_net = PlaneGather(
         wq_sems, t, lambda p: wq.at[:, p], lambda p, i: wq.at[pl.ds(2 * i, 2), p]
@@ -497,6 +504,9 @@
     wq_net.cross()
     wo_net.begin()
     hid_net.finish()
+    for y in range(GROUPS):
+        turned = hid[y].T.reshape(GROUPS, PLANE, shard, rows)
+        hid_turned[:, :, :, y * rows : (y + 1) * rows] = turned
     wq_net.finish()
 
     hidden = hid[...].reshape(many, model)
@@ -547,20 +557,15 @@
     def last(y):
         cols = pl.ds(pl.multiple_of(y * rows, rows), rows)
 
-        def step(i, carry):
-            c = pick(i, t.zxm, t.zxp, t.zxf)
+        for c in (t.zxm, t.zxp, t.zxf):
             for h in range(HEADS):
                 forward_block(kv, c, h, cols, qpad, lse, total, acc)
-            return carry
-
-        lax.fori_loop(0, 3, step, 0)
-        blocks = []
         for h in range(HEADS):
-            blocks.append((acc[h, HD : 2 * HD, cols] / total[h, :, cols]).T.astype(BF16))
+            att[h * HD : (h + 1) * HD, cols] = (
+                acc[h, HD : 2 * HD, cols] / total[h, :, cols]
+            ).astype(BF16)
             lse[h, :, cols] = lse[h, :, cols] + jnp.log(total[h, :, cols])
-        here = jnp.concatenate(blocks, axis=1)
-        att[cols, :] = here
-        part[y] = dot(here, wo16[...], 1, 0).astype(BF16)
+        part[y] = dot(att[:, cols], wo16[...], 0, 0).astype(BF16)
 
     sum_net = ColumnReduce(sum_sems, t, part, relays, lands)
     last(t.yf)
@@ -570,6 +575,15 @@
     sum_net.near()
     last(t.y)
     sum_net.relay()
+
+    def foresee(*chunks):
+        def step(i, carry):
+            prob_chunk(kv, pick(i, *chunks), qpad, lse, probs)
+            return carry
+
+        lax.fori_loop(0, len(chunks), step, 0)
+
+    foresee(t.zxf, t.zxm)
     mixed = (frames[...].astype(F32) + sum_net.finish()).astype(BF16)
 
     mixed32 = mixed.astype(F32)
@@ -580,6 +594,7 @@
     conv_edge = Edge(conv_sems, t, conv_wide)
     conv_edge.begin()
     normed_keep[...] = normed
+    foresee(t.zxp)
     conv_edge.finish()
     taps = conv_kernel.shape[0]
 
@@ -588,7 +603,7 @@
 
     def convolve(b, carry):
         lanes = lanes_of(b)
-        pre = jnp.zeros((rows, LANES), F32) + conv_bias[:, lanes]
+        pre = jnp.zeros((rows, LANES), F32) + conv_bias[lanes][None]
         for offset, moved in shifts(conv_wide[:, lanes].astype(F32), rows, taps):
             pre = pre + moved * conv_kernel[offset - 1 : offset, lanes]
         sigma = 1.0 / (1.0 + jnp.exp(-pre))
@@ -602,6 +617,7 @@
     lax.fori_loop(0, blocks, convolve, 0)
     grad_edge = Edge(grad_sems, t, grad_wide)
     grad_edge.begin()
+    foresee(t.xf)
     grad_edge.finish()
 
     def convolve_back(b, carry):
@@ -628,23 +644,26 @@
         return carry
 
     lax.fori_loop(0, blocks, kernel_grads, 0)
+    foresee(t.zo, t.xm, t.xp)
     mix_net.relay()
+    foresee(t.me)
     mix_net.finish()
 
     mixed = mix[...].reshape(many, model)
     grads = dot(mixed, wo16[...], 1, 1).astype(BF16)
+    grads_turned = dot(wo16[...], mixed, 1, 1).astype(BF16).astype(F32)
     for h in range(HEADS):
         lanes = slice(h * HD, (h + 1) * HD)
         mine = grads[:, lanes]
         dopad[h] = jnp.concatenate([zeros, mine], axis=1)
         delta[h] = jnp.sum(
-            (att[:, lanes].astype(F32) * mine.astype(F32)).T, axis=0, keepdims=True
+            att[lanes, :].astype(F32) * grads_turned[lanes, :], axis=0, keepdims=True
         )
     dqt[...] = jnp.zeros_like(dqt)
 
     def backward(*chunks):
         def step(i, carry):
-            backward_chunk(kv, pick(i, *chunks), qpad, dopad, lse, delta, dqt, dkv)
+            backward_chunk(kv, pick(i, *chunks), qpad, dopad, probs, delta, dqt, dkv)
             return carry
 
         if len(chunks) == 1:
@@ -675,7 +694,7 @@
     for h in range(HEADS):
         proj[:, h * HD : (h + 1) * HD] = (dqt[h, 0:HD, :] * HD**-0.5).T.astype(BF16)
 
-    out_terms = dot(att[...], mixed, 0, 0)
+    out_terms = dot(att[...], mixed, 1, 0)
     quarter = o_part.shape[2]
     wide = model // 2
     for c in range(2):
@@ -705,15 +724,22 @@
     red = ColumnReduce(red_sems, t, part2, relays2, lands2)
     product(t.yf)
     red.far()
-    hidden = hid[...].reshape(many, model)
     half_rows = w_part.shape[3]
-    w_terms = dot(hidden, proj[...], 0, 0).reshape(
-        GROUPS, PLANE, 2, half_rows, 3 * width
-    )
-    for c in range(2):
-        w_part[c] = w_terms[:, :, c].astype(BF16)
-    for k, p in enumerate(order):
-        pair.go(8 + k, w_part.at[1 - t.core, :, p], w_core.at[:, p], buddy)
+
+    def weight_terms(first, last):
+        for k in range(first, last):
+            p = order[k]
+            terms = dot(hid_turned[:, p].reshape(GROUPS * shard, many), proj[...], 1, 0)
+            terms = terms.reshape(GROUPS, 2, half_rows, 3 * width).astype(BF16)
+            for c in range(2):
+                w_part[c, :, p] = terms[:, c]
+            pair.go(8 + k, w_part.at[1 - t.core, :, p], w_core.at[:, p], buddy)
+
+    product(t.ym)
+    product(t.yp)
+    red.near()
+    weight_terms(0, 3)
+    product(t.y)
     w_mine, o_mine = w_part.at[t.core], o_part.at[t.core]
     o_net = PlaneReduce(
         o_sems,
@@ -739,10 +765,6 @@
             o_net.add(o_mine.at[p], o_core.at[p])
             w_net.add(w_mine.at[:, p], w_core.at[:, p])
 
-    product(t.ym)
-    product(t.yp)
-    product(t.y)
-    red.near()
     red.relay()
     join(0, 1)
     w_net.far()
@@ -750,6 +772,7 @@
     join(1, 3)
     w_net.sides()
     o_net.sides()
+    weight_terms(3, 8)
     join(3, 8)
     w_net.opposite()
     o_net.opposite()
@@ -932,7 +955,9 @@
         lse=f32(HEADS, 1, many),
         total=f32(HEADS, 1, many),
         acc=f32(HEADS, 2 * HD, many),
-        att=bf16(many, width),
+        att=bf16(width, many),
+        hid_turned=bf16(GROUPS, PLANE, shard, many),
+        probs=bf16(PLANE, HEADS, many, many),
         part=bf16(GROUPS, rows, model),
         relays=bf16(2, rows // 2, model),
         lands=bf16(2, rows, model),
@@ -1020,7 +1045,9 @@
     vmem = pl.BlockSpec(memory_space=pltpu.VMEM)
     return pl.pallas_call(
         hand_on_kernel,
-        out_shape=[jax.ShapeDtypeStruct(a.shape, a.dtype) for a in arrays],
+        out_shape=[
+            jax.ShapeDtypeStruct(a.shape[1:] if a.shape[0] == 1 else a.shape, a.dtype) for a in arrays
+        ],
         in_specs=[vmem] * len(arrays),
         out_specs=[vmem] * len(arrays),
         name="hand_on",
@@ -1030,7 +1057,7 @@
 def local(frames, w_qkv, w_out, norm_gains, conv_kernel, conv_bias, out_grad):
     block_out, grad_input, grad_qkv, grad_out, kernel_sum, bias_sum, norms_sum = hand_on(
         *whole(
-            frames[0], w_qkv, w_out, norm_gains, conv_kernel, conv_bias[None], out_grad[0]
+            frames[0], w_qkv, w_out, norm_gains, conv_kernel, conv_bias, out_grad[0]
         )
     )
     return (
@@ -1040,7 +1067,7 @@
         grad_out,
         norms_sum,
         kernel_sum,
-        bias_sum[0],
+        bias_sum,
     )
 
 

time: 190 us -> 193 us (1.016)
  Pallas kernels: 187 us -> 192 us
  local copies, waits for them, and re-layouts: 1.99 us -> 0 us
    pallas_call x1, Pallas kernels: 184 us -> 190 us  [whole(): pl.pallas_call(functools.partial(whole_kernel, names), out_shape=list(out...]
where the time goes in v1:
time: 193 us
  Pallas kernels  192 us (99%)
    pallas_call x1, Pallas kernels, whole(): pl.pallas_call(functools.partial(whole_kernel, names), out_shape=list(out...  190 us

profile of v1, /device:TPU:1, one launch (start us, length us, event | category | flops | bytes accessed | tf_op | source)
XLA Modules:
  0.0 193.0 jit_solution(9889242870427751861)
XLA Ops:
  0.6 190.1 %whole.1 = (bf16[128,1536]{1,0:T(8,128)(2,1)}, bf16[128,1536]{1,0:T(8,128)(2,1)}, bf16[48,2304]{1,0:T(8,128)(2,1)}, bf16[24,1536]{1,0:T(8,128)(2,1)}, f32[31,153...) custom-call(bf16[128,1536]{1,0:T(8,128)(2,1)} %bitcast.4, bf16[48,2304]{1,0:T(8,128)(2,1)} %refs_1_.1, ...), custom_call_target="tpu_custom_call" | custom-call | tf_op jit(solution)/shard_map/whole/pallas_call | solution.py:1025
  190.7 2.4 %hand_on.1 = (bf16[128,1536]{1,0:T(8,128)(2,1)}, bf16[128,1536]{1,0:T(8,128)(2,1)}, bf16[48,2304]{1,0:T(8,128)(2,1)}, bf16[24,1536]{1,0:T(8,128)(2,1)}, f32[31,1...) custom-call(bf16[128,1536]{1,0:T(8,128)(2,1)} %get-tuple-element.21.refs_0_, ...), custom_call_target="tpu_custom_call" | custom-call | tf_op jit(solution)/shard_map/hand_on/pallas_call | solution.py:1046

commit v2 on v1

--- a/solution.py
+++ b/solution.py
@@ -199,10 +199,10 @@
 
 
 class PlaneReduce(Wire):
-    def __init__(self, sems, place, full, half, land, half_land):
+    def __init__(self, sems, place, full, half, land, land_half, half_land):
         super().__init__(sems)
         self.at, self.full, self.half = place, full, half
-        self.land, self.half_land = land, half_land
+        self.land, self.land_half, self.half_land = land, land_half, half_land
 
     def add(self, ref, *more):
         total = ref[...].astype(F32)
@@ -212,19 +212,25 @@
 
     def far(self):
         t = self.at
-        self.go(0, self.full(t.zxf), self.land(0), t.plane(t.zo))
-
-    def sides(self):
+        self.go(0, self.half(t.zxf, 0), self.land_half(0, 0), t.plane(t.zo))
+        self.go(8, self.half(t.zxf, 1), self.land_half(0, 1), t.plane(t.zo))
+
+    def left(self):
+        self.go(1, self.full(self.at.zxm), self.land(1), self.at.plane(self.at.xm))
+
+    def right(self):
+        self.go(2, self.full(self.at.zxp), self.land(2), self.at.plane(self.at.xp))
+
+    def opposite(self, i):
         t = self.at
-        self.go(1, self.full(t.zxm), self.land(1), t.plane(t.xm))
-        self.go(2, self.full(t.zxp), self.land(2), t.plane(t.xp))
-
-    def opposite(self):
+        self.got((0, 8)[i])
+        self.add(self.half(t.xf, i), self.land_half(0, i))
+        self.go(3 + i, self.half(t.xf, i), self.half_land(i), t.plane((t.xm, t.xp)[i]))
+
+    def early(self):
         t = self.at
-        self.got(0)
-        self.add(self.full(t.xf), self.land(0))
-        self.go(3, self.half(t.xf, 0), self.half_land(0), t.plane(t.xm))
-        self.go(4, self.half(t.xf, 1), self.half_land(1), t.plane(t.xp))
+        self.go(6, self.half(t.xm, 1), self.land_half(4, 1), t.plane(t.xm))
+        self.go(7, self.half(t.xp, 0), self.land_half(5, 0), t.plane(t.xp))
 
     def across(self):
         t = self.at
@@ -236,13 +242,13 @@
         t = self.at
         self.got(3)
         self.add(self.half(t.xm, 0), self.half_land(0))
-        self.go(6, self.full(t.xm), self.land(4), t.plane(t.xm))
+        self.go(9, self.half(t.xm, 0), self.land_half(4, 0), t.plane(t.xm))
         self.got(4)
         self.add(self.half(t.xp, 1), self.half_land(1))
-        self.go(7, self.full(t.xp), self.land(5), t.plane(t.xp))
+        self.go(10, self.half(t.xp, 1), self.land_half(5, 1), t.plane(t.xp))
 
     def finish(self):
-        self.got(5, 6, 7)
+        self.got(5, 6, 7, 9, 10)
         total = self.full(self.at.me)[...].astype(F32)
         for k in (3, 4, 5):
             total = total + self.land(k)[...].astype(F32)
@@ -397,7 +403,6 @@
         total,
         acc,
         att,
-        hid_turned,
         probs,
         part,
         relays,
@@ -439,6 +444,7 @@
         s_done,
         s_fin,
         spread_sems,
+        swap_sems,
         hid_sems,
         wq_sems,
         wo_sems,
@@ -453,6 +459,7 @@
         w_sems,
         o_sems,
         hi_sems,
+        o_hi_sems,
         w_fin_send,
         w_fin_recv,
         o_fin_send,
@@ -482,32 +489,58 @@
     pl.semaphore_wait(pltpu.get_barrier_semaphore(), greeted)
     hid_net = ColumnGather(hid_sems, t, hid)
     hid_net.begin()
-    spread = Wire(spread_sems)
-    for k, y in enumerate((t.yp, t.ym, t.yf)):
-        spread.go(k, w_parts.at[y], wq.at[t.y, t.me], t.column(y))
-    wq[t.y, t.me] = w_parts[t.y]
+    holds = t.y // 2 == t.core
+    spread_copies = []
+    for k in range(1, GROUPS):
+        y = (t.y + k) % GROUPS
+        copy = pltpu.make_async_remote_copy(
+            src_ref=w_parts.at[y],
+            dst_ref=wq.at[t.y, t.me],
+            send_sem=spread_sems.at[0, k - 1],
+            recv_sem=spread_sems.at[1, k - 1],
+            device_id=t.column(y),
+        )
+        spread_copies.append((copy, ((t.y + GROUPS - k) % GROUPS) // 2 == t.core))
+
+    @pl.when(holds)
+    def _():
+        for copy, _ in spread_copies:
+            copy.start()
+        wq[t.y, t.me] = w_parts[t.y]
+
     share = width // PLANE
     wo[t.me] = jnp.concatenate(
         [w_out[...].astype(F32), jnp.zeros((wo.shape[1] - share, model), F32)], axis=0
     ).astype(BF16)
 
-    spread.got(0, 1, 2)
+    for copy, comes in spread_copies:
+        pl.when(comes)(copy.wait_recv)
+    base = 2 * t.core
     wq_net = PlaneGather(
-        wq_sems, t, lambda p: wq.at[:, p], lambda p, i: wq.at[pl.ds(2 * i, 2), p]
-    )
+        wq_sems, t, lambda p: wq.at[pl.ds(base, 2), p], lambda p, i: wq.at[base + i, p]
+    )
+    swap = Wire(swap_sems)
+    buddy = {"dp": t.hi * 2 + 1 - t.core}
+
+    def trade(*ps):
+        for p in ps:
+            half = wq.at[pl.ds(base, 2), p]
+            swap.go(len(swap.sent), half, half, buddy)
     wo_net = PlaneGather(
         wo_sems, t, lambda p: wo.at[p], lambda p, i: wo.at[p, pl.ds(16 * i, 16)]
     )
     wq_net.begin()
+    trade(t.me)
+    wq_net.relay()
+    trade(t.xm, t.xp, t.zo)
     hid_net.relay()
-    wq_net.relay()
     wq_net.cross()
+    trade(t.xf)
     wo_net.begin()
+    wq_net.finish()
+    trade(t.zxm, t.zxp, t.zxf)
     hid_net.finish()
-    for y in range(GROUPS):
-        turned = hid[y].T.reshape(GROUPS, PLANE, shard, rows)
-        hid_turned[:, :, :, y * rows : (y + 1) * rows] = turned
-    wq_net.finish()
+    swap.got(*range(PLANE))
 
     hidden = hid[...].reshape(many, model)
     weights = wq[...].reshape(model, 3 * width)
@@ -678,22 +711,9 @@
         lambda p: dkv.at[p],
         lambda p, i: dkv.at[p, pl.ds(i * half, half)],
         lambda k: kv_land.at[k],
+        lambda k, i: kv_land.at[k, pl.ds(i * half, half)],
         lambda k: kv_half.at[k],
     )
-    backward(t.zxf)
-    net.far()
-    backward(t.zxm, t.zxp)
-    net.sides()
-    backward(t.xf)
-    net.opposite()
-    backward(t.zo)
-    net.across()
-    backward(t.xm, t.xp)
-    net.near()
-    backward(t.me)
-    for h in range(HEADS):
-        proj[:, h * HD : (h + 1) * HD] = (dqt[h, 0:HD, :] * HD**-0.5).T.astype(BF16)
-
     out_terms = dot(att[...], mixed, 1, 0)
     quarter = o_part.shape[2]
     wide = model // 2
@@ -709,77 +729,106 @@
                 else:
                     piece[...] = jnp.zeros(piece.shape, BF16)
     order = (t.zxf, t.zxm, t.zxp, t.xf, t.zo, t.xm, t.xp, t.me)
-    buddy = {"dp": t.hi * 2 + 1 - t.core}
     pair = Wire(core_sems)
-    for k, p in enumerate(order):
-        pair.go(k, o_part.at[1 - t.core, p], o_core.at[p], buddy)
-    proj[:, width:] = net.finish().astype(BF16)
-
-    weights = wq[...].reshape(model, 3 * width)
-
-    def product(y):
-        here = proj[pl.ds(pl.multiple_of(y * rows, rows), rows), :]
-        part2[y] = dot(here, weights, 1, 1).astype(BF16)
-
-    red = ColumnReduce(red_sems, t, part2, relays2, lands2)
-    product(t.yf)
-    red.far()
-    half_rows = w_part.shape[3]
-
-    def weight_terms(first, last):
-        for k in range(first, last):
-            p = order[k]
-            terms = dot(hid_turned[:, p].reshape(GROUPS * shard, many), proj[...], 1, 0)
-            terms = terms.reshape(GROUPS, 2, half_rows, 3 * width).astype(BF16)
-            for c in range(2):
-                w_part[c, :, p] = terms[:, c]
-            pair.go(8 + k, w_part.at[1 - t.core, :, p], w_core.at[:, p], buddy)
-
-    product(t.ym)
-    product(t.yp)
-    red.near()
-    weight_terms(0, 3)
-    product(t.y)
-    w_mine, o_mine = w_part.at[t.core], o_part.at[t.core]
+    pair.go(16, o_part.at[1 - t.core], o_core, buddy)
+    o_mine = o_part.at[t.core]
     o_net = PlaneReduce(
         o_sems,
         t,
         lambda p: o_mine.at[p],
         lambda p, i: o_mine.at[p, pl.ds(2 * i, 2)],
         lambda k: o_land.at[k],
+        lambda k, i: o_land.at[k, pl.ds(2 * i, 2)],
         lambda k: o_half.at[k],
     )
+    backward(t.zxf)
+    net.far()
+    backward(t.zxm)
+    net.left()
+    backward(t.zxp)
+    net.right()
+    backward(t.xf)
+    net.opposite(0)
+    pair.got(16)
+    o_net.add(o_mine, o_core)
+    o_net.far()
+    backward(t.xm)
+    net.opposite(1)
+    o_net.left()
+    o_net.right()
+    backward(t.xp)
+    net.early()
+    o_net.early()
+    backward(t.zo)
+    net.across()
+    net.near()
+    o_net.opposite(0)
+    o_net.opposite(1)
+    o_net.across()
+    backward(t.me)
+    o_net.near()
+    for h in range(HEADS):
+        proj[:, h * HD : (h + 1) * HD] = (dqt[h, 0:HD, :] * HD**-0.5).T.astype(BF16)
+
+    proj[:, width:] = net.finish().astype(BF16)
+
+    weights = wq[...].reshape(model, 3 * width)
+
+    def product(y):
+        here = proj[pl.ds(pl.multiple_of(y * rows, rows), rows), :]
+        part2[y] = dot(here, weights, 1, 1).astype(BF16)
+
+    red = ColumnReduce(red_sems, t, part2, relays2, lands2)
+    product(t.yf)
+    red.far()
+    half_rows = w_part.shape[3]
+    hidden = hid[...].reshape(many, model)
+    w_terms = dot(hidden, proj[...], 0, 0).reshape(GROUPS, PLANE, 2, half_rows, 3 * width)
+    for c in range(2):
+        w_part[c] = w_terms[:, :, c].astype(BF16)
+    for k, p in enumerate(order):
+        pair.go(8 + k, w_part.at[1 - t.core, :, p], w_core.at[:, p], buddy)
+    product(t.ym)
+    product(t.yp)
+    red.near()
+    w_mine = w_part.at[t.core]
     w_net = PlaneReduce(
         w_sems,
         t,
         lambda p: w_mine.at[:, p],
         lambda p, i: w_mine.at[pl.ds(2 * i, 2), p],
         lambda k: w_land.at[k],
+        lambda k, i: w_land.at[k, pl.ds(2 * i, 2)],
         lambda k: w_half.at[k],
     )
 
     def join(first, last):
         for k in range(first, last):
             p = order[k]
-            pair.got(k, 8 + k)
-            o_net.add(o_mine.at[p], o_core.at[p])
+            pair.got(8 + k)
             w_net.add(w_mine.at[:, p], w_core.at[:, p])
 
-    red.relay()
     join(0, 1)
     w_net.far()
-    o_net.far()
-    join(1, 3)
-    w_net.sides()
-    o_net.sides()
-    weight_terms(3, 8)
-    join(3, 8)
-    w_net.opposite()
-    o_net.opposite()
+    join(1, 2)
+    w_net.left()
+    join(2, 3)
+    w_net.right()
+    product(t.y)
+    red.relay()
+    join(3, 4)
+    w_net.opposite(0)
+    w_net.opposite(1)
+    join(4, 7)
+    w_net.early()
+    o_mine[t.me] = o_net.finish().astype(BF16)
+    o_hi_net = Wire(o_hi_sems)
+    for k in range(1, 4):
+        j = (t.hi + k) % 4
+        o_hi_net.go(k - 1, o_mine.at[t.me, j], o_hi.at[k - 1], {"dp": j * 2 + t.core})
+    join(7, 8)
     w_net.across()
-    o_net.across()
     w_net.near()
-    o_net.near()
 
     grad_hidden = red.finish()
     _, normed, inverse = layer_norm(frames[...].astype(F32), gain1)
@@ -799,15 +848,32 @@
         r = (t.seq + k) % count
         s_net.go(k - 1, s_send.at[r], s_seq.at[t.seq], {"seq": r})
 
-    o_total, w_total = o_net.finish(), w_net.finish()
-    o_mine[t.me] = o_total.astype(BF16)
-    w_mine[:, t.me] = w_total.astype(BF16)
+    o_hi_net.got(0, 1, 2)
+    o_out_block = o_mine[t.me, t.hi].astype(F32)
+    for k in range(3):
+        o_out_block = o_out_block + o_hi[k].astype(F32)
+    o_done[...] = o_out_block.astype(BF16)
+    finals = []
+
+    def deliver(src, dst, send, recv, y):
+        for k in range(1, 8):
+            copy = pltpu.make_async_remote_copy(
+                src_ref=src,
+                dst_ref=dst,
+                send_sem=send.at[k],
+                recv_sem=recv,
+                device_id=t.holder(y, (t.dp + k) % 8),
+            )
+            copy.start()
+            finals.append(copy)
+
+    deliver(o_done, o_fin.at[t.hi, t.core], o_fin_send, o_fin_recv.at[t.hi, t.core], t.y)
+    w_mine[:, t.me] = w_net.finish().astype(BF16)
     hi_net = Wire(hi_sems)
     for k in range(1, 4):
         j = (t.hi + k) % 4
         there = {"dp": j * 2 + t.core}
         hi_net.go(k - 1, w_mine.at[j, t.me], w_hi.at[k - 1], there)
-        hi_net.go(2 + k, o_mine.at[t.me, j], o_hi.at[k - 1], there)
 
     s_net.got(*range(count - 1))
     s_mine[...] = jnp.sum(s_seq[...], axis=0)
@@ -816,26 +882,12 @@
     for k in range(1, 8):
         s_dp_net.go(k - 1, s_mine, s_dp.at[t.dp], {"dp": (t.dp + k) % 8})
 
-    hi_net.got(*range(6))
+    hi_net.got(*range(3))
     w_out_block = w_mine[t.hi, t.me].astype(F32)
-    o_out_block = o_mine[t.me, t.hi].astype(F32)
     for k in range(3):
         w_out_block = w_out_block + w_hi[k].astype(F32)
-        o_out_block = o_out_block + o_hi[k].astype(F32)
     w_done[...] = w_out_block.astype(BF16)
-    o_done[...] = o_out_block.astype(BF16)
-    finals = []
-    for k in range(1, 8):
-        d = (t.dp + k) % 8
-        for src, dst, send, recv, y in (
-            (w_done, w_fin.at[t.y, t.core], w_fin_send.at[k], w_fin_recv.at[t.y, t.core], t.hi),
-            (o_done, o_fin.at[t.hi, t.core], o_fin_send.at[k], o_fin_recv.at[t.hi, t.core], t.y),
-        ):
-            copy = pltpu.make_async_remote_copy(
-                src_ref=src, dst_ref=dst, send_sem=send, recv_sem=recv, device_id=t.holder(y, d)
-            )
-            copy.start()
-            finals.append(copy)
+    deliver(w_done, w_fin.at[t.y, t.core], w_fin_send, w_fin_recv.at[t.y, t.core], t.hi)
     o_own = pltpu.make_async_copy(
         o_done, o_fin.at[t.hi, t.core], o_fin_recv.at[t.hi, t.core]
     )
@@ -900,7 +952,12 @@
     def _():
         w_away.wait_send()
 
-    for wire in (spread, hid_net, wq_net, wo_net, kv_net, sum_net, mix_net, net, pair, o_net, red, w_net, hi_net, s_net, s_dp_net, s_fin_net):
+    @pl.when(holds)
+    def _():
+        for copy, _ in spread_copies:
+            copy.wait_send()
+
+    for wire in (swap, hid_net, wq_net, wo_net, kv_net, sum_net, mix_net, net, pair, o_net, red, w_net, hi_net, o_hi_net, s_net, s_dp_net, s_fin_net):
         wire.done()
 
 
@@ -956,7 +1013,6 @@
         total=f32(HEADS, 1, many),
         acc=f32(HEADS, 2 * HD, many),
         att=bf16(width, many),
-        hid_turned=bf16(GROUPS, PLANE, shard, many),
         probs=bf16(PLANE, HEADS, many, many),
         part=bf16(GROUPS, rows, model),
         relays=bf16(2, rows // 2, model),
@@ -998,6 +1054,7 @@
         s_done=f32(1, model + LANES),
         s_fin=f32(count, 1, model + LANES),
         spread_sems=wire_sems(3),
+        swap_sems=wire_sems(PLANE),
         hid_sems=wire_sems(4),
         wq_sems=wire_sems(9),
         wo_sems=wire_sems(9),
@@ -1006,12 +1063,13 @@
         conv_sems=wire_sems(2),
         grad_sems=wire_sems(2),
         mix_sems=wire_sems(4),
-        kv_sems=wire_sems(8),
+        kv_sems=wire_sems(11),
         red_sems=wire_sems(6),
-        core_sems=wire_sems(16),
-        w_sems=wire_sems(8),
-        o_sems=wire_sems(8),
-        hi_sems=wire_sems(6),
+        core_sems=wire_sems(17),
+        w_sems=wire_sems(11),
+        o_sems=wire_sems(11),
+        hi_sems=wire_sems(3),
+        o_hi_sems=wire_sems(3),
         w_fin_send=dma(8),
         w_fin_recv=dma(4, 2),
         o_fin_send=dma(8),

time: 193 us -> 191 us (0.990)
  the two profiles are of different devices: /device:TPU:1 before, /device:TPU:17 now
where the time goes in v2:
time: 191 us; the launch traced here: 187 us
  Pallas kernels  186 us (97%)
    pallas_call x1, Pallas kernels, whole(): pl.pallas_call(functools.partial(whole_kernel, names), out_shape=list(out...  184 us

profile of v2, /device:TPU:17, one launch (start us, length us, event | category | flops | bytes accessed | tf_op | source)
XLA Modules:
  0.0 186.8 jit_solution(1501424727375915368)
XLA Ops:
  0.6 183.6 %whole.1 = (bf16[128,1536]{1,0:T(8,128)(2,1)}, bf16[128,1536]{1,0:T(8,128)(2,1)}, bf16[48,2304]{1,0:T(8,128)(2,1)}, bf16[24,1536]{1,0:T(8,128)(2,1)}, f32[31,153...) custom-call(bf16[128,1536]{1,0:T(8,128)(2,1)} %bitcast.4, bf16[48,2304]{1,0:T(8,128)(2,1)} %refs_1_.1, ...), custom_call_target="tpu_custom_call" | custom-call | tf_op jit(solution)/shard_map/whole/pallas_call | solution.py:1083
  184.3 2.4 %hand_on.1 = (bf16[128,1536]{1,0:T(8,128)(2,1)}, bf16[128,1536]{1,0:T(8,128)(2,1)}, bf16[48,2304]{1,0:T(8,128)(2,1)}, bf16[24,1536]{1,0:T(8,128)(2,1)}, f32[31,1...) custom-call(bf16[128,1536]{1,0:T(8,128)(2,1)} %get-tuple-element.21.refs_0_, ...), custom_call_target="tpu_custom_call" | custom-call | tf_op jit(solution)/shard_map/hand_on/pallas_call | solution.py:1104

commit v3 on v2

--- a/solution.py
+++ b/solution.py
@@ -60,8 +60,11 @@
 
     def greet(self):
         near = [{"seq": (self.seq + i) % 32} for i in range(1, 32)]
+        near += [self.holder(self.y, (self.dp + j) % 8) for j in range(1, 8)]
         near += [
-            self.holder((self.y + i) % 4, (self.dp + j) % 8) for i in range(4) for j in range(1, 8)
+            self.holder((self.y + i) % 4, ((self.hi + j) % 4) * 2 + self.core)
+            for i in range(1, 4)
+            for j in range(1, 4)
         ]
         for device in near:
             pl.semaphore_signal(pltpu.get_barrier_semaphore(), inc=1, device_id=device)
@@ -409,6 +412,7 @@
         lands,
         mixed_keep,
         normed_keep,
+        first_keep,
         conv_wide,
         grad_wide,
         conv_back,
@@ -460,6 +464,7 @@
         o_sems,
         hi_sems,
         o_hi_sems,
+        cross_sems,
         w_fin_send,
         w_fin_recv,
         o_fin_send,
@@ -484,7 +489,8 @@
                 columns.append(w_qkv[:, start : start + HD])
         w_parts[g] = jnp.concatenate(columns, axis=1)
     inputs = frames[...].astype(F32)
-    shifted, _, _ = layer_norm(inputs, gain1)
+    shifted, normed, inverse1 = layer_norm(inputs, gain1)
+    first_keep[...] = normed
     hid[t.y] = shifted.astype(BF16)
     pl.semaphore_wait(pltpu.get_barrier_semaphore(), greeted)
     hid_net = ColumnGather(hid_sems, t, hid)
@@ -509,9 +515,13 @@
         wq[t.y, t.me] = w_parts[t.y]
 
     share = width // PLANE
-    wo[t.me] = jnp.concatenate(
-        [w_out[...].astype(F32), jnp.zeros((wo.shape[1] - share, model), F32)], axis=0
-    ).astype(BF16)
+    wide = model // 2
+    for c in range(2):
+
+        @pl.when(t.core == c)
+        def _(c=c):
+            wo[c, t.me] = w_out[:, c * wide : (c + 1) * wide]
+
 
     for copy, comes in spread_copies:
         pl.when(comes)(copy.wait_recv)
@@ -527,7 +537,10 @@
             half = wq.at[pl.ds(base, 2), p]
             swap.go(len(swap.sent), half, half, buddy)
     wo_net = PlaneGather(
-        wo_sems, t, lambda p: wo.at[p], lambda p, i: wo.at[p, pl.ds(16 * i, 16)]
+        wo_sems,
+        t,
+        lambda p: wo.at[t.core, p],
+        lambda p, i: wo.at[t.core, p, :, pl.ds(i * (wide // 2), wide // 2)],
     )
     wq_net.begin()
     trade(t.me)
@@ -581,8 +594,11 @@
     wo_net.cross()
     attend(t.xf)
     wo_net.finish()
+    swap.go(PLANE, wo.at[t.core], wo.at[t.core], buddy)
+    swap.got(PLANE)
     for p in range(PLANE):
-        wo32[p * share : (p + 1) * share, :] = wo[p, 0:share, :].astype(F32)
+        for c in range(2):
+            wo32[p * share : (p + 1) * share, c * wide : (c + 1) * wide] = wo[c, p].astype(F32)
     wo16[...] = wo32[...].astype(BF16)
     kv_net.got(5, 6)
     kv_net.got(7, 8)
@@ -714,9 +730,15 @@
         lambda k, i: kv_land.at[k, pl.ds(i * half, half)],
         lambda k: kv_half.at[k],
     )
+    order = (t.zxf, t.zxm, t.zxp, t.xf, t.zo, t.xm, t.xp, t.me)
+    backward(t.zxm)
+    net.left()
+    backward(t.zxp)
+    net.right()
+    backward(t.zxf)
+    net.far()
     out_terms = dot(att[...], mixed, 1, 0)
     quarter = o_part.shape[2]
-    wide = model // 2
     for c in range(2):
         for p in range(PLANE):
             for i in range(quarter):
@@ -728,7 +750,6 @@
                     ].astype(BF16)
                 else:
                     piece[...] = jnp.zeros(piece.shape, BF16)
-    order = (t.zxf, t.zxm, t.zxp, t.xf, t.zo, t.xm, t.xp, t.me)
     pair = Wire(core_sems)
     pair.go(16, o_part.at[1 - t.core], o_core, buddy)
     o_mine = o_part.at[t.core]
@@ -741,23 +762,17 @@
         lambda k, i: o_land.at[k, pl.ds(2 * i, 2)],
         lambda k: o_half.at[k],
     )
-    backward(t.zxf)
-    net.far()
-    backward(t.zxm)
-    net.left()
-    backward(t.zxp)
-    net.right()
     backward(t.xf)
-    net.opposite(0)
     pair.got(16)
     o_net.add(o_mine, o_core)
     o_net.far()
-    backward(t.xm)
-    net.opposite(1)
     o_net.left()
     o_net.right()
+    backward(t.xm)
+    net.opposite(0)
     backward(t.xp)
     net.early()
+    net.opposite(1)
     o_net.early()
     backward(t.zo)
     net.across()
@@ -831,8 +846,7 @@
     w_net.near()
 
     grad_hidden = red.finish()
-    _, normed, inverse = layer_norm(frames[...].astype(F32), gain1)
-    norm_grad, gain_sum = norm_back(grad_hidden, normed, inverse, gain1)
+    norm_grad, gain_sum = norm_back(grad_hidden, first_keep[...], inverse1, gain1)
     grad_input[...] = (mix[t.y].astype(F32) + norm_grad).astype(BF16)
     gains = (gain_sum[None], gain2_grad)
     count = s_send.shape[0]
@@ -856,18 +870,22 @@
     finals = []
 
     def deliver(src, dst, send, recv, y):
-        for k in range(1, 8):
+        for k in range(1, 4):
             copy = pltpu.make_async_remote_copy(
                 src_ref=src,
                 dst_ref=dst,
                 send_sem=send.at[k],
                 recv_sem=recv,
-                device_id=t.holder(y, (t.dp + k) % 8),
+                device_id=t.holder(y, ((t.hi + k) % 4) * 2 + t.core),
             )
             copy.start()
             finals.append(copy)
 
     deliver(o_done, o_fin.at[t.hi, t.core], o_fin_send, o_fin_recv.at[t.hi, t.core], t.y)
+    o_own = pltpu.make_async_copy(
+        o_done, o_fin.at[t.hi, t.core], o_fin_recv.at[t.hi, t.core]
+    )
+    o_own.start()
     w_mine[:, t.me] = w_net.finish().astype(BF16)
     hi_net = Wire(hi_sems)
     for k in range(1, 4):
@@ -888,10 +906,6 @@
         w_out_block = w_out_block + w_hi[k].astype(F32)
     w_done[...] = w_out_block.astype(BF16)
     deliver(w_done, w_fin.at[t.y, t.core], w_fin_send, w_fin_recv.at[t.y, t.core], t.hi)
-    o_own = pltpu.make_async_copy(
-        o_done, o_fin.at[t.hi, t.core], o_fin_recv.at[t.hi, t.core]
-    )
-    o_own.start()
     w_own = pltpu.make_async_copy(w_done, w_fin.at[t.y, t.core], w_fin_recv.at[t.y, t.core])
     w_away = pltpu.make_async_remote_copy(
         src_ref=w_done,
@@ -919,10 +933,14 @@
     for k in range(1, count):
         s_fin_net.go(k - 1, s_done, s_fin.at[t.seq], {"seq": (t.seq + k) % count})
 
+    cross = Wire(cross_sems)
     for i in range(4):
-        for c in range(2):
-            pltpu.make_async_copy(w_done, w_fin.at[i, c], w_fin_recv.at[i, c]).wait()
-            pltpu.make_async_copy(o_done, o_fin.at[i, c], o_fin_recv.at[i, c]).wait()
+        pltpu.make_async_copy(o_done, o_fin.at[i, t.core], o_fin_recv.at[i, t.core]).wait()
+        cross.go(i, o_fin.at[i, t.core], o_fin.at[i, t.core], buddy)
+    for i in range(4):
+        pltpu.make_async_copy(w_done, w_fin.at[i, t.core], w_fin_recv.at[i, t.core]).wait()
+        cross.go(4 + i, w_fin.at[i, t.core], w_fin.at[i, t.core], buddy)
+    cross.got(*range(8))
     pieces = [w_fin[y].astype(F32).reshape(2 * half_rows, 3 * width) for y in range(GROUPS)]
     columns = [piece[:, :width] for piece in pieces]
     for kind in range(2):
@@ -957,7 +975,7 @@
         for copy, _ in spread_copies:
             copy.wait_send()
 
-    for wire in (swap, hid_net, wq_net, wo_net, kv_net, sum_net, mix_net, net, pair, o_net, red, w_net, hi_net, o_hi_net, s_net, s_dp_net, s_fin_net):
+    for wire in (swap, hid_net, wq_net, wo_net, kv_net, sum_net, mix_net, net, pair, o_net, red, w_net, hi_net, o_hi_net, cross, s_net, s_dp_net, s_fin_net):
         wire.done()
 
 
@@ -979,7 +997,6 @@
     many = GROUPS * rows
     width = HEADS * HD
     half = shard // 2
-    padded = 32
     count = conv_kernel.shape[0] + 1
     like = jax.ShapeDtypeStruct
     ins = dict(
@@ -1004,7 +1021,7 @@
         w_parts=bf16(GROUPS, shard, 3 * width),
         hid=bf16(GROUPS, rows, model),
         wq=bf16(GROUPS, PLANE, shard, 3 * width),
-        wo=bf16(PLANE, padded, model),
+        wo=bf16(2, PLANE, width // PLANE, model // 2),
         wo32=f32(width, model),
         wo16=bf16(width, model),
         kv=bf16(PLANE, many, 2 * width),
@@ -1019,6 +1036,7 @@
         lands=bf16(2, rows, model),
         mixed_keep=f32(rows, model),
         normed_keep=f32(rows, model),
+        first_keep=f32(rows, model),
         conv_wide=bf16(rows + 2 * HALO, model),
         grad_wide=bf16(rows + 2 * HALO, model),
         conv_back=f32(rows, model),
@@ -1054,7 +1072,7 @@
         s_done=f32(1, model + LANES),
         s_fin=f32(count, 1, model + LANES),
         spread_sems=wire_sems(3),
-        swap_sems=wire_sems(PLANE),
+        swap_sems=wire_sems(PLANE + 1),
         hid_sems=wire_sems(4),
         wq_sems=wire_sems(9),
         wo_sems=wire_sems(9),
@@ -1070,6 +1088,7 @@
         o_sems=wire_sems(11),
         hi_sems=wire_sems(3),
         o_hi_sems=wire_sems(3),
+        cross_sems=wire_sems(8),
         w_fin_send=dma(8),
         w_fin_recv=dma(4, 2),
         o_fin_send=dma(8),

time: 191 us -> 192 us (level)
  the two profiles are of different devices: /device:TPU:17 before, /device:TPU:1 now
where the time goes in v3:
time: 192 us; the launch traced here: 188 us
  Pallas kernels  187 us (97%)
    pallas_call x1, Pallas kernels, whole(): pl.pallas_call(functools.partial(whole_kernel, names), out_shape=list(out...  185 us

profile of v3, /device:TPU:1, one launch (start us, length us, event | category | flops | bytes accessed | tf_op | source)
XLA Modules:
  0.0 188.3 jit_solution(10500311500327334901)
XLA Ops:
  0.6 185.1 %whole.1 = (bf16[128,1536]{1,0:T(8,128)(2,1)}, bf16[128,1536]{1,0:T(8,128)(2,1)}, bf16[48,2304]{1,0:T(8,128)(2,1)}, bf16[24,1536]{1,0:T(8,128)(2,1)}, f32[31,153...) custom-call(bf16[128,1536]{1,0:T(8,128)(2,1)} %bitcast.4, bf16[48,2304]{1,0:T(8,128)(2,1)} %refs_1_.1, ...), custom_call_target="tpu_custom_call" | custom-call | tf_op jit(solution)/shard_map/whole/pallas_call | solution.py:1102
  185.7 2.4 %hand_on.1 = (bf16[128,1536]{1,0:T(8,128)(2,1)}, bf16[128,1536]{1,0:T(8,128)(2,1)}, bf16[48,2304]{1,0:T(8,128)(2,1)}, bf16[24,1536]{1,0:T(8,128)(2,1)}, f32[31,1...) custom-call(bf16[128,1536]{1,0:T(8,128)(2,1)} %get-tuple-element.21.refs_0_, ...), custom_call_target="tpu_custom_call" | custom-call | tf_op jit(solution)/shard_map/hand_on/pallas_call | solution.py:1123

commit v4 on v3

--- a/solution.py
+++ b/solution.py
@@ -469,6 +469,13 @@
         w_fin_recv,
         o_fin_send,
         o_fin_recv,
+        g_mine,
+        g_y,
+        g_plane_mine,
+        g_plane,
+        g_dp_mine,
+        g_dp,
+        g_sems,
         s_sems,
         s_dp_sems,
         s_fin_sems,
@@ -762,6 +769,17 @@
         lambda k, i: o_land.at[k, pl.ds(2 * i, 2)],
         lambda k: o_half.at[k],
     )
+    count = s_send.shape[0]
+    for r in range(count):
+        if r < model // LANES:
+            s_send[r, :, model:] = gain2_grad[:, r * LANES : (r + 1) * LANES]
+        else:
+            s_send[r, :, model:] = jnp.zeros((1, LANES), F32)
+    s_net = Wire(s_sems)
+    s_seq[t.seq] = s_send[t.seq]
+    for k in range(1, count):
+        r = (t.seq + k) % count
+        s_net.go(k - 1, s_send.at[r], s_seq.at[t.seq], {"seq": r})
     backward(t.xf)
     pair.got(16)
     o_net.add(o_mine, o_core)
@@ -773,6 +791,13 @@
     backward(t.xp)
     net.early()
     net.opposite(1)
+    s_net.got(*range(count - 1))
+    s_mine[...] = jnp.sum(s_seq[...], axis=0)
+    s_dp[t.dp] = s_mine[...]
+    s_dp_net = Wire(s_dp_sems)
+    for k in range(1, 8):
+        s_dp_net.go(k - 1, s_mine, s_dp.at[t.dp], {"dp": (t.dp + k) % 8})
+
     o_net.early()
     backward(t.zo)
     net.across()
@@ -782,6 +807,16 @@
     o_net.across()
     backward(t.me)
     o_net.near()
+    s_dp_net.got(*range(7))
+    summed = s_dp[0]
+    for d in range(1, 8):
+        summed = summed + s_dp[d]
+    s_done[...] = summed
+    s_fin[t.seq] = summed
+    s_fin_net = Wire(s_fin_sems)
+    for k in range(1, count):
+        s_fin_net.go(k - 1, s_done, s_fin.at[t.seq], {"seq": (t.seq + k) % count})
+
     for h in range(HEADS):
         proj[:, h * HD : (h + 1) * HD] = (dqt[h, 0:HD, :] * HD**-0.5).T.astype(BF16)
 
@@ -845,22 +880,23 @@
     w_net.across()
     w_net.near()
 
+    s_fin_net.got(*range(count - 1))
+    for r in range(count):
+        row = s_fin[r]
+        if r < taps:
+            kernel_sum[r : r + 1, :] = row[:, :model]
+        else:
+            bias_sum[...] = row[:, :model]
+        if r < model // LANES:
+            norms_sum[1:2, r * LANES : (r + 1) * LANES] = row[:, model:]
     grad_hidden = red.finish()
     norm_grad, gain_sum = norm_back(grad_hidden, first_keep[...], inverse1, gain1)
     grad_input[...] = (mix[t.y].astype(F32) + norm_grad).astype(BF16)
-    gains = (gain_sum[None], gain2_grad)
-    count = s_send.shape[0]
-    for r in range(count):
-        if r < 2 * (model // 128):
-            row, col = divmod(r, model // 128)
-            s_send[r, :, model:] = gains[row][:, col * 128 : (col + 1) * 128]
-        else:
-            s_send[r, :, model:] = jnp.zeros((1, 128), F32)
-    s_net = Wire(s_sems)
-    s_seq[t.seq] = s_send[t.seq]
-    for k in range(1, count):
-        r = (t.seq + k) % count
-        s_net.go(k - 1, s_send.at[r], s_seq.at[t.seq], {"seq": r})
+    g_mine[...] = gain_sum[None]
+    g_y[t.y] = g_mine[...]
+    g_net = Wire(g_sems)
+    for k, y in enumerate((t.yp, t.ym, t.yf)):
+        g_net.go(k, g_mine, g_y.at[t.y], t.column(y))
 
     o_hi_net.got(0, 1, 2)
     o_out_block = o_mine[t.me, t.hi].astype(F32)
@@ -893,12 +929,11 @@
         there = {"dp": j * 2 + t.core}
         hi_net.go(k - 1, w_mine.at[j, t.me], w_hi.at[k - 1], there)
 
-    s_net.got(*range(count - 1))
-    s_mine[...] = jnp.sum(s_seq[...], axis=0)
-    s_dp[t.dp] = s_mine[...]
-    s_dp_net = Wire(s_dp_sems)
-    for k in range(1, 8):
-        s_dp_net.go(k - 1, s_mine, s_dp.at[t.dp], {"dp": (t.dp + k) % 8})
+    g_net.got(0, 1, 2)
+    g_plane_mine[...] = ((g_y[0] + g_y[1]) + g_y[2]) + g_y[3]
+    g_plane[t.me] = g_plane_mine[...]
+    for k in range(1, PLANE):
+        g_net.go(2 + k, g_plane_mine, g_plane.at[t.me], t.plane((t.me + k) % PLANE))
 
     hi_net.got(*range(3))
     w_out_block = w_mine[t.hi, t.me].astype(F32)
@@ -923,15 +958,14 @@
     def _():
         w_away.start()
 
-    s_dp_net.got(*range(7))
-    summed = s_dp[0]
-    for d in range(1, 8):
-        summed = summed + s_dp[d]
-    s_done[...] = summed
-    s_fin[t.seq] = summed
-    s_fin_net = Wire(s_fin_sems)
-    for k in range(1, count):
-        s_fin_net.go(k - 1, s_done, s_fin.at[t.seq], {"seq": (t.seq + k) % count})
+    g_net.got(*range(3, 10))
+    along = g_plane[0]
+    for p in range(1, PLANE):
+        along = along + g_plane[p]
+    g_dp_mine[...] = along
+    g_dp[t.dp] = along
+    for k in range(1, 8):
+        g_net.go(9 + k, g_dp_mine, g_dp.at[t.dp], {"dp": (t.dp + k) % 8})
 
     cross = Wire(cross_sems)
     for i in range(4):
@@ -953,16 +987,11 @@
         o_fin[0 : share // 8, c].astype(F32).reshape(share, wide) for c in range(2)
     ]
     grad_out[...] = jnp.concatenate(sides, axis=1).astype(BF16)
-    s_fin_net.got(*range(count - 1))
-    for r in range(count):
-        row = s_fin[r]
-        if r < taps:
-            kernel_sum[r : r + 1, :] = row[:, :model]
-        else:
-            bias_sum[...] = row[:, :model]
-        if r < 2 * (model // 128):
-            i, col = divmod(r, model // 128)
-            norms_sum[i : i + 1, col * 128 : (col + 1) * 128] = row[:, model:]
+    g_net.got(*range(10, 17))
+    along = g_dp[0]
+    for d in range(1, 8):
+        along = along + g_dp[d]
+    norms_sum[0:1, :] = along
     for copy in finals:
         copy.wait_send()
 
@@ -975,7 +1004,7 @@
         for copy, _ in spread_copies:
             copy.wait_send()
 
-    for wire in (swap, hid_net, wq_net, wo_net, kv_net, sum_net, mix_net, net, pair, o_net, red, w_net, hi_net, o_hi_net, cross, s_net, s_dp_net, s_fin_net):
+    for wire in (swap, hid_net, wq_net, wo_net, kv_net, sum_net, mix_net, net, pair, o_net, red, w_net, hi_net, o_hi_net, cross, s_net, s_dp_net, s_fin_net, g_net):
         wire.done()
 
 
@@ -1093,6 +1122,13 @@
         w_fin_recv=dma(4, 2),
         o_fin_send=dma(8),
         o_fin_recv=dma(4, 2),
+        g_mine=f32(1, model),
+        g_y=f32(GROUPS, 1, model),
+        g_plane_mine=f32(1, model),
+        g_plane=f32(PLANE, 1, model),
+        g_dp_mine=f32(1, model),
+        g_dp=f32(8, 1, model),
+        g_sems=wire_sems(17),
         s_sems=wire_sems(count - 1),
         s_dp_sems=wire_sems(7),
         s_fin_sems=wire_sems(count - 1),

time: 192 us -> 191 us (level)
  no operation moved by 1% of the time
where the time goes in v4:
time: 191 us; the launch traced here: 187 us
  Pallas kernels  186 us (97%)
    pallas_call x1, Pallas kernels, whole(): pl.pallas_call(functools.partial(whole_kernel, names), out_shape=list(out...  184 us

profile of v4, /device:TPU:1, one launch (start us, length us, event | category | flops | bytes accessed | tf_op | source)
XLA Modules:
  0.0 187.1 jit_solution(17553417182718931937)
XLA Ops:
  0.6 183.8 %whole.1 = (bf16[128,1536]{1,0:T(8,128)(2,1)}, bf16[128,1536]{1,0:T(8,128)(2,1)}, bf16[48,2304]{1,0:T(8,128)(2,1)}, bf16[24,1536]{1,0:T(8,128)(2,1)}, f32[31,153...) custom-call(bf16[128,1536]{1,0:T(8,128)(2,1)} %bitcast.4, bf16[48,2304]{1,0:T(8,128)(2,1)} %refs_1_.1, ...), custom_call_target="tpu_custom_call" | custom-call | tf_op jit(solution)/shard_map/whole/pallas_call | solution.py:1138
  184.5 2.4 %hand_on.1 = (bf16[128,1536]{1,0:T(8,128)(2,1)}, bf16[128,1536]{1,0:T(8,128)(2,1)}, bf16[48,2304]{1,0:T(8,128)(2,1)}, bf16[24,1536]{1,0:T(8,128)(2,1)}, f32[31,1...) custom-call(bf16[128,1536]{1,0:T(8,128)(2,1)} %get-tuple-element.21.refs_0_, ...), custom_call_target="tpu_custom_call" | custom-call | tf_op jit(solution)/shard_map/hand_on/pallas_call | solution.py:1159
